TPU v7x, 128 devices: a whole 4x4x4 slice. The times are simulated.
128 devices in a mesh: pts: 32 (over x, y, core), code: 4 (over z).
Axes of the slice: x: 4, y: 4, z: 4, core: 2. Of those that a mesh axis runs over, the one named last changes fastest.
Arguments:
- features: bfloat16 [32768, 512], P('pts'), may hold values from -18 to 18
- codebook: bfloat16 [16384, 512], P('code'), may hold values from -0.25 to 0.25
Outputs:
- new_codes: bfloat16 [16384, 512], P('code')
- row_potential: float32 [32768], P('pts')
- column_potential: float32 [16384], P('code')
All inputs are finite; a program needn't handle non-finite values.
Results may differ from a plain program's by a relative error of at most 0.0051.
Values may be sent and summed in bfloat16 or wider, within the bound.
No kernel may reach another device: no remote copies, remote signals or barrier semaphores. Data moves between devices by JAX's collectives and lax.ppermute only.
A program may use at most 128 MiB of HBM per device.

v0:
```python
import math

import jax
import jax.numpy as jnp
from jax import lax
from jax.sharding import PartitionSpec as P

ITERS = 3


def merged(value, axis, combine):
    everything = jax.tree.map(lambda part: lax.all_gather(part, axis), value)
    leading = jax.tree.map(lambda part: part[0], everything)

    def lap(k, so_far):
        return combine(so_far, jax.tree.map(lambda part: part[k], everything))

    return lax.fori_loop(1, lax.axis_size(axis), lap, leading)


def combine_lse(earlier, later):
    peak_val = jnp.maximum(earlier[0], later[0])
    total = earlier[1] * jnp.exp(earlier[0] - peak_val) + later[1] * jnp.exp(later[0] - peak_val)
    return (peak_val, total)


def per_device(features, codebook):
    logits = lax.dot_general(
        features, codebook, (((1,), (1,)), ((), ())), preferred_element_type=jnp.float32
    )
    row_count = logits.shape[0]
    col_count = logits.shape[1]
    total_rows = row_count * lax.axis_size("pts")
    total_codes = col_count * lax.axis_size("code")
    target_mass = math.log(total_rows / total_codes)
    row_pot = jnp.zeros((row_count,), jnp.float32)
    col_pot = jnp.zeros((col_count,), jnp.float32)
    for iteration in range(ITERS):
        shifted = logits + row_pot[:, None]
        col_peak = lax.pmax(jnp.max(shifted, axis=0), "pts")
        col_total = lax.psum(jnp.sum(jnp.exp(shifted - col_peak[None, :]), axis=0), "pts")
        col_pot = target_mass - (col_peak + jnp.log(col_total))
        shifted = logits + col_pot[None, :]
        local_max = jnp.max(shifted, axis=1)
        local_sum = jnp.sum(jnp.exp(shifted - local_max[:, None]), axis=1)
        row_peak, row_total = merged((local_max, local_sum), "code", combine_lse)
        row_pot = -(row_peak + jnp.log(row_total))
    plan = jnp.exp(logits + row_pot[:, None] + col_pot[None, :])
    local_mass = jnp.sum(plan, axis=0)
    plan_half = plan.astype(jnp.bfloat16)
    local_numer = lax.dot_general(
        plan_half, features, (((0,), (0,)), ((), ())), preferred_element_type=jnp.float32
    )
    numer, mass_total = lax.psum((local_numer, local_mass), "pts")
    new_codes = (numer / mass_total[:, None]).astype(jnp.bfloat16)
    return (new_codes, row_pot, col_pot)


def solution(mesh):
    return jax.shard_map(
        per_device,
        mesh=mesh,
        in_specs=(P("pts", None), P("code", None)),
        out_specs=(P("code", None), P("pts"), P("code")),
        check_vma=False,
    )
```

profile of v0, /device:TPU:0, one launch (start us, length us, event | category | flops | bytes accessed | tf_op | source)
XLA Modules:
  0.0 1089.8 jit_solution(3298286350729547193)
XLA Ops:
  7.2 0.0 copy-start
  7.2 0.0 all-reduce.2.cloned.1.call-start
  7.2 1.2 copy-done
  8.4 10.3 fusion.6
  18.7 128.5 %pmax.21 = f32[4096]{0:T(1024)S(1)} all-reduce(f32[4096]{0:T(1024)S(1)} %get-tuple-element.450), channel_id=1, replica_groups=mesh['pts'=32,'code'=4] {'pts'}, use_global_device_ids=true, to_apply=%region_1.0 | all-reduce | flops 4096 | bytes 32768 | tf_op jit(solution)/shard_map/pmax | solution.py:40
  147.1 8.0 exponential_reduce_fusion.5
  155.1 123.8 %psum.35 = f32[4096]{0:T(1024)S(1)} all-reduce(f32[4096]{0:T(1024)S(1)} %exponential_reduce_fusion.5), channel_id=1, replica_groups=mesh['pts'=32,'code'=4] {'pts'}, use_global_device_ids=true, to_apply=%region_3.0 | all-reduce | flops 4096 | bytes 32768 | tf_op jit(solution)/shard_map/psum | solution.py:41
  278.9 7.1 add_reduce_fusion.4
  286.0 8.7 exponential_reduce_fusion.4
  294.7 13.1 %all-gather = f32[4096]{0:T(1024)S(1)} all-gather(f32[1024]{0:T(1024)S(1)} %add_reduce_fusion.4), channel_id=2, replica_groups=mesh['pts'=32,'code'=4] {'code'}, dimensions={0}, use_global_device_ids=true | all-gather | bytes 20480 | tf_op jit(solution)/shard_map/all_gather | solution.py:12
  307.9 11.9 %all-gather.1 = f32[4096]{0:T(1024)S(1)} all-gather(f32[1024]{0:T(1024)S(1)} %exponential_reduce_fusion.4), channel_id=3, replica_groups=mesh['pts'=32,'code'=4] {'code'}, dimensions={0}, use_global_device_ids=true | all-gather | bytes 20480 | tf_op jit(solution)/shard_map/all_gather | solution.py:12
  319.8 0.2 while.51
  320.0 7.2 add_reduce_fusion.3
  327.2 124.2 %pmax.22 = f32[4096]{0:T(1024)S(1)} all-reduce(f32[4096]{0:T(1024)S(1)} %add_reduce_fusion.3), channel_id=1, replica_groups=mesh['pts'=32,'code'=4] {'pts'}, use_global_device_ids=true, to_apply=%region_9.0 | all-reduce | flops 4096 | bytes 32768 | tf_op jit(solution)/shard_map/pmax | solution.py:40
  451.4 9.2 exponential_reduce_fusion.3
  460.6 123.8 %psum.36 = f32[4096]{0:T(1024)S(1)} all-reduce(f32[4096]{0:T(1024)S(1)} %exponential_reduce_fusion.3), channel_id=1, replica_groups=mesh['pts'=32,'code'=4] {'pts'}, use_global_device_ids=true, to_apply=%region_11.0 | all-reduce | flops 4096 | bytes 32768 | tf_op jit(solution)/shard_map/psum | solution.py:41
  584.4 7.1 add_reduce_fusion.2
  591.5 8.7 exponential_reduce_fusion.2
  600.2 11.9 %all-gather.2 = f32[4096]{0:T(1024)S(1)} all-gather(f32[1024]{0:T(1024)S(1)} %add_reduce_fusion.2), channel_id=4, replica_groups=mesh['pts'=32,'code'=4] {'code'}, dimensions={0}, use_global_device_ids=true | all-gather | bytes 20480 | tf_op jit(solution)/shard_map/all_gather | solution.py:12
  612.2 11.9 %all-gather.3 = f32[4096]{0:T(1024)S(1)} all-gather(f32[1024]{0:T(1024)S(1)} %exponential_reduce_fusion.2), channel_id=5, replica_groups=mesh['pts'=32,'code'=4] {'code'}, dimensions={0}, use_global_device_ids=true | all-gather | bytes 20480 | tf_op jit(solution)/shard_map/all_gather | solution.py:12
  624.1 0.2 while.52
  624.3 7.2 add_reduce_fusion.1
  631.5 123.9 %pmax.23 = f32[4096]{0:T(1024)S(1)} all-reduce(f32[4096]{0:T(1024)S(1)} %add_reduce_fusion.1), channel_id=1, replica_groups=mesh['pts'=32,'code'=4] {'pts'}, use_global_device_ids=true, to_apply=%region_17.0 | all-reduce | flops 4096 | bytes 32768 | tf_op jit(solution)/shard_map/pmax | solution.py:40
  755.4 9.2 exponential_reduce_fusion.1
  764.7 123.8 %psum.37 = f32[4096]{0:T(1024)S(1)} all-reduce(f32[4096]{0:T(1024)S(1)} %exponential_reduce_fusion.1), channel_id=1, replica_groups=mesh['pts'=32,'code'=4] {'pts'}, use_global_device_ids=true, to_apply=%region_19.0 | all-reduce | flops 4096 | bytes 32768 | tf_op jit(solution)/shard_map/psum | solution.py:41
  888.4 0.0 copy-start.1
  888.5 6.9 add_reduce_fusion
  895.4 8.6 exponential_reduce_fusion
  904.0 11.9 %all-gather.4 = f32[4096]{0:T(1024)S(1)} all-gather(f32[1024]{0:T(1024)S(1)} %add_reduce_fusion), channel_id=6, replica_groups=mesh['pts'=32,'code'=4] {'code'}, dimensions={0}, use_global_device_ids=true | all-gather | bytes 20480 | tf_op jit(solution)/shard_map/all_gather | solution.py:12
  916.0 12.1 %all-gather.5 = f32[4096]{0:T(1024)S(1)} all-gather(f32[1024]{0:T(1024)S(1)} %exponential_reduce_fusion), channel_id=7, replica_groups=mesh['pts'=32,'code'=4] {'code'}, dimensions={0}, use_global_device_ids=true | all-gather | bytes 20480 | tf_op jit(solution)/shard_map/all_gather | solution.py:12
  928.1 0.2 while.53
  928.3 0.0 copy-start.2
  928.3 14.2 %fusion.2 = f32[4096,512]{1,0:T(8,128)} fusion(bf16[1024,512]{1,0:T(8,128)(2,1)S(1)} %copy-done, f32[1024,4096]{1,0:T(8,128)} %get-tuple-element.451, f32[1024]{0:T(1024)S(1)} %add_negate_fusion, f32[4096]{0:T(1024)S(1)} %add_subtract_fusion), kind=kOutput, calls=%fused_computation.23 | convolution fusion | flops 4307550208 | bytes 26234880 | tf_op jit(solution)/shard_map/dot_general | solution.py:51
  942.5 0.0 all-reduce.2.cloned.1.call-update
  942.5 0.0 copy-done.1
  942.6 0.0 copy-done.2
  942.6 10.0 fusion
  952.6 125.0 %psum.39 = f32[4096]{0:T(1024)S(1)} all-reduce(f32[4096]{0:T(1024)S(1)} %fusion), channel_id=1, replica_groups=mesh['pts'=32,'code'=4] {'pts'}, use_global_device_ids=true, to_apply=%region_26.0 | all-reduce | flops 4096 | bytes 32768 | tf_op jit(solution)/shard_map/psum | solution.py:54
  1077.6 0.0 all-reduce.2.cloned.1.call-done
  1077.6 5.2 divide_convert_fusion
  (36 shorter events, 0.3 us)
Async XLA Ops:
  7.2 1.2 copy-start
  7.2 1070.4 %all-reduce.2.cloned.1.call-start = ((), (), s32[]{:S(2)}) async-start(), calls=%async_computation | async-start | bytes 16777216 | tf_op jit(solution)/shard_map/psum | solution.py:54
  888.4 54.1 %copy-start.1 = (f32[4096]{0:T(1024)}, f32[4096]{0:T(1024)S(1)}, u32[]{:S(2)}) copy-start(f32[4096]{0:T(1024)S(1)} %add_subtract_fusion) | copy-start | bytes 49156
  928.3 14.2 %copy-start.2 = (f32[1024]{0:T(1024)}, f32[1024]{0:T(1024)S(1)}, u32[]{:S(2)}) copy-start(f32[1024]{0:T(1024)S(1)} %add_negate_fusion) | copy-start | bytes 12292
Sparse Core Ops, SparseCore 0:
  942.7 116.7 all-reduce.1
where the time goes:
time: 1100 us; the launch traced here: 1090 us
  blocking collectives  946 us (86%)
  other arithmetic  103 us (9%)
  matrix products  24.5 us (2%)
  between operations  14.4 us (1%)
    pmax x3, blocking collectives, per_device(): col_peak = lax.pmax(jnp.max(shifted, axis=0), 'pts')  377 us
    psum x3, blocking collectives, per_device(): lax.psum(jnp.sum(jnp.exp(shifted - col_peak[None, :]), axis=0), 'pts')  371 us
    psum x1, blocking collectives, per_device(): numer, mass_total = lax.psum((local_numer, local_mass), 'pts')  125 us
    all_gather x6, blocking collectives, merged(): everything = jax.tree.map(lambda part: lax.all_gather(part, axis), value)  73 us
    reduce_sum x3, other arithmetic, per_device(): jnp.sum(jnp.exp(shifted - col_peak[None, :]), axis=0)  26.5 us
    reduce_sum x3, other arithmetic, per_device(): local_sum = jnp.sum(jnp.exp(shifted - local_max[:, None]), axis=1)  26.1 us
  transfers between devices with their start and end apart: 1, of which 0 were waited for; matrix products, arithmetic and copies ran while one was open for 1% of the time, Pallas kernels for 0%

commit v1 on v0

v1 whole, which is shorter than its diff:
```python
import functools
import math

import jax
import jax.numpy as jnp
from jax import lax
from jax.experimental import pallas as pl
from jax.experimental.pallas import tpu as pltpu
from jax.sharding import PartitionSpec as P

BF = jnp.bfloat16
F32 = jnp.float32
VMEM = 48 * 1024 * 1024
NT = (((1,), (1,)), ((), ()))
NN = (((1,), (0,)), ((), ()))


def place(x, y, c):
    return ((x % 4) * 4 + (y % 4)) * 2 + c


def shift(value, move):
    pairs = []
    for x in range(4):
        for y in range(4):
            for c in range(2):
                pairs.append((place(x, y, c), place(*move(x, y, c))))
    return lax.ppermute(value, "pts", pairs)


def along_x(value, d):
    return shift(value, lambda x, y, c: (x + d, y, c))


def along_y(value, d):
    return shift(value, lambda x, y, c: (x, y + d, c))


def other_core(value):
    return shift(value, lambda x, y, c: (x, y, 1 - c))


def first_axis(value, d):
    return shift(value, lambda x, y, c: (x + d * c, y + d * (1 - c), c))


def second_axis(value, d):
    return shift(value, lambda x, y, c: (x + d * (1 - c), y + d * c, c))


def params():
    return pltpu.CompilerParams(vmem_limit_bytes=VMEM)


def lse_of(parts):
    peak = functools.reduce(jnp.maximum, parts)
    return peak + jnp.log(sum(jnp.exp(p - peak) for p in parts))


def split_rows(v):
    n = v.shape[1]
    hi = v.astype(BF).astype(F32)
    mid = (v - hi).astype(BF).astype(F32)
    low = v - hi - mid
    row = lax.broadcasted_iota(jnp.int32, (16, n), 0)
    return jnp.where(row == 0, hi, jnp.where(row == 1, mid, jnp.where(row == 2, low, 0.0))).astype(BF)


def to_row(col):
    n = col.shape[0]
    diag = lax.broadcasted_iota(jnp.int32, (128, 128), 0) == lax.broadcasted_iota(jnp.int32, (128, 128), 1)
    parts = []
    for i in range(0, n, 128):
        parts.append(jnp.sum(jnp.where(diag, col[i : i + 128], 0.0), axis=0, keepdims=True))
    return jnp.concatenate(parts, axis=1)


def columns(core, feats, codebook, codes, bc=256):
    rows = feats.shape[0]

    def kern(core_ref, f_ref, c_ref, o_ref):
        logits = lax.dot_general(f_ref[...], c_ref[...], NT, preferred_element_type=F32)
        peak = jnp.max(logits, axis=0, keepdims=True)
        o_ref[...] = peak + jnp.log(jnp.sum(jnp.exp(logits - peak), axis=0, keepdims=True))

    return pl.pallas_call(
        kern,
        out_shape=jax.ShapeDtypeStruct((1, codes), F32),
        grid_spec=pltpu.PrefetchScalarGridSpec(
            num_scalar_prefetch=1,
            grid=(codes // bc,),
            in_specs=[
                pl.BlockSpec((rows, feats.shape[1]), lambda j, core: (0, 0)),
                pl.BlockSpec((bc, feats.shape[1]), lambda j, core: (core[0] * (codes // bc) + j, 0)),
            ],
            out_specs=pl.BlockSpec((1, bc), lambda j, core: (0, j)),
        ),
        compiler_params=params(),
        name="columns",
    )(core, feats, codebook)


def rows_first(core, feats, codebook, parts, target, codes, rb=256):
    rows, width = feats.shape

    def kern(core_ref, f_ref, c_ref, p0, p1, p2, p3, a_ref, lse_ref, peak_ref, col_ref):
        @pl.when(pl.program_id(0) == 0)
        def _():
            col_ref[...] = target - lse_of([p0[...], p1[...], p2[...], p3[...]])

        for s in range(0, rb, 128):
            val = lax.dot_general(f_ref[pl.ds(s, 128), :], c_ref[...], NT, preferred_element_type=F32) + col_ref[...]
            peak = jnp.max(val, axis=1, keepdims=True)
            ex = jnp.exp(val - peak)
            total = jnp.sum(ex, axis=1, keepdims=True)
            a_ref[pl.ds(s, 128), :] = ex.astype(BF)
            lse_ref[:, :, pl.ds(s, 128)] = jnp.broadcast_to(to_row(peak + jnp.log(total))[None], (8, 1, 128))
            peak_ref[:, pl.ds(s, 128)] = to_row(peak)

    vec = pl.BlockSpec((1, codes), lambda i, core: (0, 0))
    return pl.pallas_call(
        kern,
        out_shape=(
            jax.ShapeDtypeStruct((rows, codes), BF),
            jax.ShapeDtypeStruct((8, 1, rows), F32),
            jax.ShapeDtypeStruct((1, rows), F32),
            jax.ShapeDtypeStruct((1, codes), F32),
        ),
        grid_spec=pltpu.PrefetchScalarGridSpec(
            num_scalar_prefetch=1,
            grid=(rows // rb,),
            in_specs=[
                pl.BlockSpec((rb, width), lambda i, core: (i, 0)),
                pl.BlockSpec((codes, width), lambda i, core: (core[0], 0)),
                vec, vec, vec, vec,
            ],
            out_specs=(
                pl.BlockSpec((rb, codes), lambda i, core: (i, 0)),
                pl.BlockSpec((8, 1, rb), lambda i, core: (0, 0, i)),
                pl.BlockSpec((1, rb), lambda i, core: (0, i)),
                vec,
            ),
        ),
        compiler_params=params(),
        name="rows_first",
    )(core, feats, codebook, *parts)


def col_sums_first(scaled, lses, peak, rb=512):
    rows, codes = scaled.shape

    def kern(a_ref, l_ref, p_ref, s_ref, r_ref, w_ref, lhs):
        i = pl.program_id(0)

        @pl.when(i == 0)
        def _():
            pot = -lse_of([l_ref[k] for k in range(8)])
            weight = jnp.exp(p_ref[...] + pot)
            r_ref[...] = pot
            w_ref[...] = weight
            for b in range(rows // rb):
                lhs[b] = split_rows(weight[:, b * rb : (b + 1) * rb])
            s_ref[...] = jnp.zeros_like(s_ref)

        out = lax.dot_general(lhs[i], a_ref[...], NN, preferred_element_type=F32)
        s_ref[...] += jnp.sum(out, axis=0, keepdims=True)

    return pl.pallas_call(
        kern,
        out_shape=(
            jax.ShapeDtypeStruct((1, codes), F32),
            jax.ShapeDtypeStruct((1, rows), F32),
            jax.ShapeDtypeStruct((1, rows), F32),
        ),
        grid=(rows // rb,),
        in_specs=[
            pl.BlockSpec((rb, codes), lambda i: (i, 0)),
            pl.BlockSpec((8, 1, rows), lambda i: (0, 0, 0)),
            pl.BlockSpec((1, rows), lambda i: (0, 0)),
        ],
        out_specs=(
            pl.BlockSpec((1, codes), lambda i: (0, 0)),
            pl.BlockSpec((1, rows), lambda i: (0, 0)),
            pl.BlockSpec((1, rows), lambda i: (0, 0)),
        ),
        scratch_shapes=[pltpu.VMEM((rows // rb, 16, rb), BF)],
        compiler_params=params(),
        name="col_sums_first",
    )(scaled, lses, peak)


def col_sums(scaled, totals, weight, rb=512):
    rows, codes = scaled.shape

    def kern(a_ref, t_ref, w_ref, s_ref, lhs):
        i = pl.program_id(0)

        @pl.when(i == 0)
        def _():
            rho = w_ref[...] / sum(t_ref[k] for k in range(8))
            for b in range(rows // rb):
                lhs[b] = split_rows(rho[:, b * rb : (b + 1) * rb])
            s_ref[...] = jnp.zeros_like(s_ref)

        out = lax.dot_general(lhs[i], a_ref[...], NN, preferred_element_type=F32)
        s_ref[...] += jnp.sum(out, axis=0, keepdims=True)

    return pl.pallas_call(
        kern,
        out_shape=jax.ShapeDtypeStruct((1, codes), F32),
        grid=(rows // rb,),
        in_specs=[
            pl.BlockSpec((rb, codes), lambda i: (i, 0)),
            pl.BlockSpec((8, 1, rows), lambda i: (0, 0, 0)),
            pl.BlockSpec((1, rows), lambda i: (0, 0)),
        ],
        out_specs=pl.BlockSpec((1, codes), lambda i: (0, 0)),
        scratch_shapes=[pltpu.VMEM((rows // rb, 16, rb), BF)],
        compiler_params=params(),
        name="col_sums",
    )(scaled, totals, weight)


def row_sums(scaled, weight, parts, first_col, scale, rb=512):
    rows, codes = scaled.shape

    def kern(a_ref, w_ref, p0, p1, p2, p3, c_ref, t_ref, col_ref, lhs):
        @pl.when(pl.program_id(0) == 0)
        def _():
            ratio = scale / (p0[...] + p1[...] + p2[...] + p3[...])
            col_ref[...] = c_ref[...] + jnp.log(ratio)
            lhs[...] = split_rows(ratio)

        out = lax.dot_general(lhs[...], a_ref[...], NT, preferred_element_type=F32)
        total = jnp.sum(out, axis=0, keepdims=True) * w_ref[...]
        t_ref[...] = jnp.broadcast_to(total[None], t_ref.shape)

    vec = pl.BlockSpec((1, codes), lambda i: (0, 0))
    return pl.pallas_call(
        kern,
        out_shape=(jax.ShapeDtypeStruct((8, 1, rows), F32), jax.ShapeDtypeStruct((1, codes), F32)),
        grid=(rows // rb,),
        in_specs=[
            pl.BlockSpec((rb, codes), lambda i: (i, 0)),
            pl.BlockSpec((1, rb), lambda i: (0, i)),
            vec, vec, vec, vec, vec,
        ],
        out_specs=(pl.BlockSpec((8, 1, rb), lambda i: (0, 0, i)), vec),
        scratch_shapes=[pltpu.VMEM((16, codes), BF)],
        compiler_params=params(),
        name="row_sums",
    )(scaled, weight, *parts, first_col)


def weigh(feats_t, totals, weight, first_row, lb=512):
    width, rows = feats_t.shape

    def kern(f_ref, t_ref, w_ref, r_ref, lhs_ref, row_ref):
        total = sum(t_ref[k] for k in range(8))
        rho = w_ref[...] / total
        row_ref[...] = r_ref[...] - jnp.log(total)
        lhs_ref[pl.ds(0, width), :] = (f_ref[...].astype(F32) * rho).astype(BF)
        lhs_ref[pl.ds(width, 16), :] = split_rows(rho)

    return pl.pallas_call(
        kern,
        out_shape=(jax.ShapeDtypeStruct((width + 16, rows), BF), jax.ShapeDtypeStruct((1, rows), F32)),
        grid=(rows // lb,),
        in_specs=[
            pl.BlockSpec((width, lb), lambda i: (0, i)),
            pl.BlockSpec((8, 1, lb), lambda i: (0, 0, i)),
            pl.BlockSpec((1, lb), lambda i: (0, i)),
            pl.BlockSpec((1, lb), lambda i: (0, i)),
        ],
        out_specs=(pl.BlockSpec((width + 16, lb), lambda i: (0, i)), pl.BlockSpec((1, lb), lambda i: (0, i))),
        compiler_params=params(),
        name="weigh",
    )(feats_t, totals, weight, first_row)


def mass_rows(mass):
    hi = mass.astype(BF).astype(F32)
    row = lax.broadcasted_iota(jnp.int32, (16, mass.shape[1]), 0)
    return jnp.where(row == 0, hi, jnp.where(row == 1, mass - hi, 0.0))


def numerators(chunk, lhs, scaled, dtype, lanes, nb=256):
    height, rows = lhs.shape
    width = height - 16

    def kern(chunk_ref, l_ref, a_ref, o_ref):
        out = lax.dot_general(l_ref[...], a_ref[...], NN, preferred_element_type=F32)
        mass = jnp.sum(out[width:], axis=0, keepdims=True)
        o_ref[pl.ds(0, width), :] = out[:width].astype(dtype)
        o_ref[pl.ds(width, 16), :] = mass_rows(mass).astype(dtype)

    per = lanes // nb
    return pl.pallas_call(
        kern,
        out_shape=jax.ShapeDtypeStruct((height, lanes), dtype),
        grid_spec=pltpu.PrefetchScalarGridSpec(
            num_scalar_prefetch=1,
            grid=(per,),
            in_specs=[
                pl.BlockSpec((height, rows), lambda j, chunk: (0, 0)),
                pl.BlockSpec((rows, nb), lambda j, chunk: (0, chunk[0] * per + j)),
            ],
            out_specs=pl.BlockSpec((height, nb), lambda j, chunk: (0, j)),
        ),
        compiler_params=params(),
        name="numerators",
    )(chunk, lhs, scaled)


def add_first(position, own, arrived):
    height, lanes = own.shape
    width = height - 16
    piece = lanes // 4

    def kern(pos_ref, own_ref, r1, r2, r3, *outs):
        for d in range(4):
            at = pl.ds(pl.multiple_of(lax.rem(pos_ref[0] + d, 4) * piece, piece), piece)
            total = own_ref[:, at]
            for r in (r1, r2, r3):
                total = total + r[:, at].astype(F32)
            mass = jnp.sum(total[width:], axis=0, keepdims=True)
            outs[d][pl.ds(0, width), :] = total[:width].astype(outs[d].dtype)
            outs[d][pl.ds(width, 16), :] = mass_rows(mass).astype(outs[d].dtype)

    whole = pl.BlockSpec(memory_space=pltpu.VMEM)
    return pl.pallas_call(
        kern,
        out_shape=[jax.ShapeDtypeStruct((height, piece), F32 if d == 0 else BF) for d in range(4)],
        in_specs=[pl.BlockSpec(memory_space=pltpu.SMEM)] + [whole] * 4,
        out_specs=[whole] * 4,
        compiler_params=params(),
        name="add_first",
    )(position, own, *arrived)


def add_second(own, arrived):
    height, lanes = own.shape
    width = height - 16

    def kern(own_ref, r1, r2, r3, o_ref):
        total = own_ref[...]
        for r in (r1, r2, r3):
            total = total + r[...].astype(F32)
        mass = jnp.sum(total[width:], axis=0, keepdims=True)
        o_ref[...] = (total[:width] / mass).T.astype(BF)

    whole = pl.BlockSpec(memory_space=pltpu.VMEM)
    return pl.pallas_call(
        kern,
        out_shape=jax.ShapeDtypeStruct((lanes, width), BF),
        in_specs=[whole] * 4,
        out_specs=whole,
        compiler_params=params(),
        name="add_second",
    )(own, *arrived)


def per_device(features, codebook):
    me = lax.axis_index("pts")
    core = me % 2
    x, y = me // 8, (me // 2) % 4
    codes = codebook.shape[0] // 2
    total_rows = features.shape[0] * lax.axis_size("pts")
    total_codes = codebook.shape[0] * lax.axis_size("code")
    target = math.log(total_rows / total_codes)
    core_arr = core.astype(jnp.int32).reshape(1)

    theirs = other_core(features)
    lse_own = columns(core_arr, features, codebook, codes)
    lse_their = columns(core_arr, theirs, codebook, codes)
    feats = jnp.where(core == 0, jnp.stack([features, theirs]), jnp.stack([theirs, features]))
    feats = feats.reshape(-1, features.shape[1])
    feats_t = feats.T

    def across(value):
        group = [
            [place(a, b, c) * 4 + z for c in range(2) for z in range(4)]
            for a in range(4) for b in range(4)
        ]
        return lax.all_to_all(value, ("pts", "code"), 0, 0, tiled=True, axis_index_groups=group)

    def around(value, move):
        return [value] + [move(value, d) for d in (1, 2, 3)]

    lse = lse_of(around(lse_of([lse_own, lse_their]), along_x))
    scaled, lses, peak, first_col = rows_first(core_arr, feats, codebook, around(lse, along_y), target, codes)
    sums, first_row, weight = col_sums_first(scaled, across(lses), peak)
    sums = sum(around(sums, along_x))
    totals, _ = row_sums(scaled, weight, around(sums, along_y), first_col, math.exp(target))
    sums = col_sums(scaled, across(totals), weight)
    sums = sum(around(sums, along_x))
    totals, col_pot = row_sums(scaled, weight, around(sums, along_y), first_col, math.exp(target))
    lhs, row_pot = weigh(feats_t, across(totals), weight, first_row)

    at_first = jnp.where(core == 0, y, x)
    at_second = jnp.where(core == 0, x, y)
    their_first = jnp.where(core == 0, x, y)
    quarter = codes // 4

    def chunk(d):
        return ((at_first + d) % 4).astype(jnp.int32).reshape(1)

    arrived = []
    for d in (2, 1, 3):
        arrived.append(first_axis(numerators(chunk(d), lhs, scaled, BF, quarter), d))
    own = numerators(chunk(0), lhs, scaled, F32, quarter)
    pieces = add_first(at_second.astype(jnp.int32).reshape(1), own, arrived)
    arrived = [second_axis(pieces[d], d) for d in (2, 1, 3)]
    fresh = add_second(pieces[0], arrived)

    piece = quarter // 4
    part = jnp.zeros((quarter, fresh.shape[1]), BF)
    for d in range(4):
        got = fresh if d == 0 else second_axis(fresh, d)
        part = lax.dynamic_update_slice(part, got, (((at_second - d) % 4) * piece, 0))
    out = jnp.zeros(codebook.shape, BF)
    for d in (2, 1, 3, 0):
        got = part if d == 0 else first_axis(part, d)
        out = lax.dynamic_update_slice(out, got, (core * codes + ((at_first - d) % 4) * quarter, 0))
        got = other_core(got)
        out = lax.dynamic_update_slice(out, got, ((1 - core) * codes + ((their_first - d) % 4) * quarter, 0))

    half = row_pot.shape[1] // 2
    my_rows = lax.dynamic_slice(row_pot.reshape(-1), (core * half,), (half,))
    their_col = other_core(col_pot)
    cols = jnp.where(core == 0, jnp.stack([col_pot, their_col]), jnp.stack([their_col, col_pot])).reshape(-1)
    return out, my_rows, cols


def solution(mesh):
    return jax.shard_map(
        per_device,
        mesh=mesh,
        in_specs=(P("pts", None), P("code", None)),
        out_specs=(P("code", None), P("pts"), P("code")),
        check_vma=False,
    )
```

time: 1100 us -> 202 us (0.18)
  the two profiles are of different devices: /device:TPU:0 before, /device:TPU:3 now
where the time goes in v1:
time: 202 us; the launch traced here: 201 us
  starting transfers between devices  67.9 us (34%)
  Pallas kernels  64.5 us (32%)
  waiting for transfers between devices  30.8 us (15%)
  blocking collectives  23.3 us (12%)
  local copies, waits for them, and re-layouts  10.7 us (5%)
  other arithmetic  2.75 us (1%)
    ppermute x36, starting transfers between devices, shift(): return lax.ppermute(value, 'pts', pairs)  61.1 us
    ppermute x36, waiting for transfers between devices, shift(): return lax.ppermute(value, 'pts', pairs)  28.3 us
    all_to_all x2, blocking collectives, across(): lax.all_to_all(value, ('pts', 'code'), 0, 0, tiled=True, axis_index_group...  23.3 us
    pallas_call x1, Pallas kernels, rows_first(): pl.pallas_call(kern, out_shape=(jax.ShapeDtypeStruct((rows, codes), BF),...  17.2 us
    pallas_call x2, Pallas kernels, row_sums(): pl.pallas_call(kern, out_shape=(jax.ShapeDtypeStruct((8, 1, rows), F32),...  12.1 us
    pallas_call x4, Pallas kernels, numerators(): pl.pallas_call(kern, out_shape=jax.ShapeDtypeStruct((height, lanes), dtyp...  11.7 us
    pallas_call x2, Pallas kernels, columns(): pl.pallas_call(kern, out_shape=jax.ShapeDtypeStruct((1, codes), F32), gri...  11.1 us
    unnamed x14, local copies, waits for them, and re-layouts  7.02 us
  transfers between devices with their start and end apart: 37, of which 18 were waited for; matrix products, arithmetic and copies ran while one was open for 3% of the time, Pallas kernels for 7%

profile of v1, /device:TPU:3, one launch (start us, length us, event | category | flops | bytes accessed | tf_op | source)
XLA Modules:
  0.0 200.9 jit_solution(1186518108769457878)
XLA Ops:
  1.4 2.2 %copy-done = bf16[4096,512]{1,0:T(8,128)(2,1)S(1)} copy-done((bf16[4096,512]{1,0:T(8,128)(2,1)S(1)}, bf16[4096,512]{1,0:T(8,128)(2,1)}, u32[]{:S(2)}) %copy-start) | copy-done | bytes 4194328
  4.8 5.6 %columns.2 = f32[1,2048]{1,0:T(1,128)S(1)} custom-call(s32[1]{0:T(128)} %bitcast.6.core_ref, bf16[1024,512]{1,0:T(8,128)(2,1)S(1)} %copy-done.3, bf16[4096,512]{1,0:T(8,128)(2,1)S(1)} %copy-done), custom_call_target="tpu_custom_call" | custom-call | tf_op jit(solution)/shard_map/columns/pallas_call | solution.py:86
  10.4 5.6 %columns.3 = f32[1,2048]{1,0:T(1,128)S(1)} custom-call(s32[1]{0:T(128)} %bitcast.6.core_ref, bf16[1024,512]{1,0:T(8,128)(2,1)S(1)} %collective-permute-done.f_ref, bf16[4096,512]{1,0:T(8,128)(2,1)S(1)} %copy-done.1), custom_call_target="tpu_custom_call" | custom-call | tf_op jit(solution)/shard_map/columns/pallas_call | solution.py:86
  16.0 1.3 collective-permute-start.1
  18.1 2.0 collective-permute-start.3
  20.0 1.3 collective-permute-done.2
  21.4 1.4 collective-permute-start.4
  22.8 2.6 %collective-permute-start.5 = (f32[1,2048]{1,0:T(1,128)S(1)}, f32[1,2048]{1,0:T(1,128)S(1)}, u32[]{:S(2)}, u32[]{:S(2)}) collective-permute-start(f32[1,2048]{1,0:T(1,128)S(1)} %log_add_fusion.p0), channel_id=1, source_target_pairs={{0,16},{4,20},{8,24},{12,28},{16,0},{20,4},{24,8},{28,12},{32,48},... | collective-permute-start | bytes 24584 | tf_op jit(solution)/shard_map/ppermute | solution.py:28
  26.5 2.0 maximum_select_fusion
  28.5 17.2 %rows_first.1 = (bf16[2048,2048]{1,0:T(8,128)(2,1)}, f32[8,1,2048]{2,1,0:T(1,128)S(1)}, f32[1,2048]{1,0:T(1,128)S(1)}, f32[1,2048]{1,0:T(1,128)S(1)}) custom-call(s32[1]{0:T(128)} %bitcast.6.core_ref, bf16[2048,512]{1,0:T(8,128)(2,1)S(1)} %bitcast.14, bf16[4096,512]{1,0:T(8,128)(2,1)} %c_ref.5, f32[1,2048]{1,0:T(1,128)S(1)} %log_add_fusion.p0, ...), custom_call_target="tpu_custom_call" | custom-call | tf_op jit(solution)/shard_map/rows_first/pallas_call | solution.py:121
  45.7 12.6 %all_to_all.15.l_ref = f32[8,1,2048]{2,1,0:T(1,128)S(1)} all-to-all(f32[8,1,2048]{2,1,0:T(1,128)S(1)} %get-tuple-element.20), channel_id=1, replica_groups={{0,1,2,3,4,5,6,7},{8,9,10,11,12,13,14,15},{16,17,18,19,20,21,22,23},{24..., dimensions={0} | all-to-all | bytes 131072 | tf_op jit(solution)/shard_map/all_to_all | solution.py:385
  58.3 4.8 %col_sums_first.1 = (f32[1,2048]{1,0:T(1,128)S(1)}, f32[1,2048]{1,0:T(1,128)S(1)}, f32[1,2048]{1,0:T(1,128)S(1)}) custom-call(bf16[2048,2048]{1,0:T(8,128)(2,1)} %get-tuple-element.19.a_ref, f32[8,1,2048]{2,1,0:T(1,128)S(1)} %all_to_all.15.l_ref, f32[1,2048]{1,0:T(1,128)S(1)} %get-tuple-element.21.p_ref), custom_call_target="tpu_custom_call" | custom-call | tf_op jit(solution)/shard_map/col_sums_first/pallas_call | solution.py:168
  64.1 2.4 %collective-permute-start.8 = (f32[1,2048]{1,0:T(1,128)S(1)}, f32[1,2048]{1,0:T(1,128)S(1)}, u32[]{:S(2)}, u32[]{:S(2)}) collective-permute-start(f32[1,2048]{1,0:T(1,128)S(1)} %get-tuple-element.23), channel_id=1, source_target_pairs={{0,64},{4,68},{8,72},{12,76},{16,80},{20,84},{24,88},{28,92},{32,9... | collective-permute-start | bytes 24584 | tf_op jit(solution)/shard_map/ppermute | solution.py:28
  66.5 1.8 collective-permute-start.9
  69.5 3.3 %collective-permute-start.11 = (f32[1,2048]{1,0:T(1,128)S(1)}, f32[1,2048]{1,0:T(1,128)S(1)}, u32[]{:S(2)}, u32[]{:S(2)}) collective-permute-start(f32[1,2048]{1,0:T(1,128)S(1)} %add_add_fusion.1.p0), channel_id=1, source_target_pairs={{0,16},{4,20},{8,24},{12,28},{16,0},{20,4},{24,8},{28,12},{32,48},... | collective-permute-start | bytes 24584 | tf_op jit(solution)/shard_map/ppermute | solution.py:28
  73.9 1.7 collective-permute-done.12.p3
  75.6 6.0 %row_sums.2 = (f32[8,1,2048]{2,1,0:T(1,128)S(1)}, f32[1,2048]{1,0:T(1,128)}) custom-call(bf16[2048,2048]{1,0:T(8,128)(2,1)} %get-tuple-element.19.a_ref, f32[1,2048]{1,0:T(1,128)S(1)} %get-tuple-element.22.w_ref, f32[1,2048]{1,0:T(1,128)S(1)} %add_add_fusion.1.p0, f32[1,2048]{1,0:T(1,128)S(1)} %collective-permute-done.10.p1, ...), custom_call_target="tpu_custom_call" | custom-call | tf_op jit(solution)/shard_map/row_sums/pallas_call | solution.py:239
  81.7 10.7 %all_to_all.16.t_ref = f32[8,1,2048]{2,1,0:T(1,128)S(1)} all-to-all(f32[8,1,2048]{2,1,0:T(1,128)S(1)} %get-tuple-element.25), channel_id=1, replica_groups={{0,1,2,3,4,5,6,7},{8,9,10,11,12,13,14,15},{16,17,18,19,20,21,22,23},{24..., dimensions={0} | all-to-all | bytes 131072 | tf_op jit(solution)/shard_map/all_to_all | solution.py:385
  92.3 4.8 %col_sums.1 = f32[1,2048]{1,0:T(1,128)S(1)} custom-call(bf16[2048,2048]{1,0:T(8,128)(2,1)} %get-tuple-element.19.a_ref, f32[8,1,2048]{2,1,0:T(1,128)S(1)} %all_to_all.16.t_ref, f32[1,2048]{1,0:T(1,128)S(1)} %get-tuple-element.22.w_ref), custom_call_target="tpu_custom_call" | custom-call | tf_op jit(solution)/shard_map/col_sums/pallas_call | solution.py:208
  97.2 1.3 collective-permute-start.13
  98.4 2.3 %collective-permute-start.14 = (f32[1,2048]{1,0:T(1,128)S(1)}, f32[1,2048]{1,0:T(1,128)S(1)}, u32[]{:S(2)}, u32[]{:S(2)}) collective-permute-start(f32[1,2048]{1,0:T(1,128)S(1)} %col_sums.1), channel_id=1, source_target_pairs={{0,64},{4,68},{8,72},{12,76},{16,80},{20,84},{24,88},{28,92},{32,9... | collective-permute-start | bytes 24584 | tf_op jit(solution)/shard_map/ppermute | solution.py:28
  101.1 1.3 collective-permute-done.14
  103.7 2.2 %collective-permute-start.17 = (f32[1,2048]{1,0:T(1,128)S(1)}, f32[1,2048]{1,0:T(1,128)S(1)}, u32[]{:S(2)}, u32[]{:S(2)}) collective-permute-start(f32[1,2048]{1,0:T(1,128)S(1)} %add_add_fusion.p0), channel_id=1, source_target_pairs={{0,16},{4,20},{8,24},{12,28},{16,0},{20,4},{24,8},{28,12},{32,48},... | collective-permute-start | bytes 24584 | tf_op jit(solution)/shard_map/ppermute | solution.py:28
  108.4 6.0 %row_sums.3 = (f32[8,1,2048]{2,1,0:T(1,128)}, f32[1,2048]{1,0:T(1,128)S(1)}) custom-call(bf16[2048,2048]{1,0:T(8,128)(2,1)} %get-tuple-element.19.a_ref, f32[1,2048]{1,0:T(1,128)S(1)} %get-tuple-element.22.w_ref, f32[1,2048]{1,0:T(1,128)S(1)} %add_add_fusion.p0, f32[1,2048]{1,0:T(1,128)S(1)} %collective-permute-done.16.p1, ...), custom_call_target="tpu_custom_call" | custom-call | tf_op jit(solution)/shard_map/row_sums/pallas_call | solution.py:239
  114.5 6.8 %all-to-all-start.2 = ((f32[8,1,2048]{2,1,0:T(1,128)}), f32[8,1,2048]{2,1,0:T(1,128)S(1)}, u32[]{:S(2)}, u32[]{:S(2)}) async-start(f32[8,1,2048]{2,1,0:T(1,128)} %get-tuple-element.26), calls=%async_computation.2 | async-start | bytes 131072 | tf_op jit(solution)/shard_map/all_to_all | solution.py:385
  121.2 2.4 %copy.7 = bf16[2048,512]{0,1:T(8,128)(2,1)} copy(bf16[2048,512]{1,0:T(8,128)(2,1)S(1)} %bitcast.15) | data formatting | bytes 4194304 | tf_op jit(solution)/shard_map/jit(_where)/select_n | solution.py:376
  123.6 2.6 %all-to-all-done.2.t_ref = f32[8,1,2048]{2,1,0:T(1,128)S(1)} async-done(((f32[8,1,2048]{2,1,0:T(1,128)}), f32[8,1,2048]{2,1,0:T(1,128)S(1)}, u32[]{:S(2)}, u32[]{:S(2)}) %all-to-all-start.2) | async-done | bytes 65568 | tf_op jit(solution)/shard_map/all_to_all | solution.py:385
  126.2 1.6 copy-done.2
  128.6 2.8 %numerators.7 = bf16[528,512]{1,0:T(8,128)(2,1)S(1)} custom-call(s32[1]{0:T(128)} %bitcast.9.chunk_ref, bf16[528,2048]{1,0:T(8,128)(2,1)S(1)} %get-tuple-element.28.l_ref, bf16[2048,2048]{1,0:T(8,128)(2,1)} %get-tuple-element.19.a_ref), custom_call_target="tpu_custom_call" | custom-call | tf_op jit(solution)/shard_map/numerators/pallas_call | solution.py:298
  131.8 2.8 %numerators.6 = bf16[528,512]{1,0:T(8,128)(2,1)S(1)} custom-call(s32[1]{0:T(128)} %bitcast.8.chunk_ref, bf16[528,2048]{1,0:T(8,128)(2,1)S(1)} %get-tuple-element.28.l_ref, bf16[2048,2048]{1,0:T(8,128)(2,1)} %get-tuple-element.19.a_ref), custom_call_target="tpu_custom_call" | custom-call | tf_op jit(solution)/shard_map/numerators/pallas_call | solution.py:298
  135.7 3.4 %numerators.5 = bf16[528,512]{1,0:T(8,128)(2,1)} custom-call(s32[1]{0:T(128)} %bitcast.7.chunk_ref, bf16[528,2048]{1,0:T(8,128)(2,1)S(1)} %get-tuple-element.28.l_ref, bf16[2048,2048]{1,0:T(8,128)(2,1)} %get-tuple-element.19.a_ref), custom_call_target="tpu_custom_call" | custom-call | tf_op jit(solution)/shard_map/numerators/pallas_call | solution.py:298
  139.2 3.0 %collective-permute-start.19 = (bf16[528,512]{1,0:T(8,128)(2,1)}, bf16[528,512]{1,0:T(8,128)(2,1)}, u32[]{:S(2)}, u32[]{:S(2)}) collective-permute-start(bf16[528,512]{1,0:T(8,128)(2,1)} %numerators.5), channel_id=1, source_target_pairs={{0,16},{4,68},{8,24},{12,76},{16,0},{20,84},{24,8},{28,92},{32,48}... | collective-permute-start | bytes 1622024 | tf_op jit(solution)/shard_map/ppermute | solution.py:28
  142.2 2.8 %numerators.4.own_ref = f32[528,512]{1,0:T(8,128)S(1)} custom-call(s32[1]{0:T(128)} %bitcast.1.chunk_ref, bf16[528,2048]{1,0:T(8,128)(2,1)S(1)} %get-tuple-element.28.l_ref, bf16[2048,2048]{1,0:T(8,128)(2,1)} %get-tuple-element.19.a_ref), custom_call_target="tpu_custom_call" | custom-call | tf_op jit(solution)/shard_map/numerators/pallas_call | solution.py:298
  145.0 4.5 %collective-permute-done.19.r1 = bf16[528,512]{1,0:T(8,128)(2,1)} collective-permute-done((bf16[528,512]{1,0:T(8,128)(2,1)}, bf16[528,512]{1,0:T(8,128)(2,1)}, u32[]{:S(2)}, u32[]{:S(2)}) %collective-permute-start.19) | collective-permute-done | bytes 540704 | tf_op jit(solution)/shard_map/ppermute | solution.py:28
  149.6 1.7 add_first.1
  151.3 1.3 collective-permute-start.22
  152.6 1.6 collective-permute-start.23
  155.3 1.5 collective-permute-done.22.r1
  156.8 1.4 collective-permute-done.23.r2
  158.4 1.4 collective-permute-start.25
  159.7 2.1 %collective-permute-start.26 = (bf16[128,512]{1,0:T(8,128)(2,1)S(1)}, bf16[128,512]{1,0:T(8,128)(2,1)S(1)}, u32[]{:S(2)}, u32[]{:S(2)}) collective-permute-start(bf16[128,512]{1,0:T(8,128)(2,1)S(1)} %add_second.1), channel_id=1, source_target_pairs={{0,64},{4,20},{8,72},{12,28},{16,80},{20,4},{24,88},{28,12},{32,96... | collective-permute-start | bytes 393224 | tf_op jit(solution)/shard_map/ppermute | solution.py:28
  163.5 2.2 %collective-permute-done.26 = bf16[128,512]{1,0:T(8,128)(2,1)S(1)} collective-permute-done((bf16[128,512]{1,0:T(8,128)(2,1)S(1)}, bf16[128,512]{1,0:T(8,128)(2,1)S(1)}, u32[]{:S(2)}, u32[]{:S(2)}) %collective-permute-start.26) | collective-permute-done | bytes 131104 | tf_op jit(solution)/shard_map/ppermute | solution.py:28
  165.7 3.6 %collective-permute-start.28 = (bf16[512,512]{1,0:T(8,128)(2,1)S(1)}, bf16[512,512]{1,0:T(8,128)(2,1)S(1)}, u32[]{:S(2)}, u32[]{:S(2)}) collective-permute-start(bf16[512,512]{1,0:T(8,128)(2,1)S(1)} %constant_dynamic-update-slice_fusion.8), channel_id=1, source_target_pairs={{0,16},{4,68},{8,24},{12,76},{16,0},{20,84},{24,8},{28,92},{32,48}... | collective-permute-start | bytes 1572872 | tf_op jit(solution)/shard_map/ppermute | solution.py:28
  170.8 6.9 %collective-permute-done.28 = bf16[512,512]{1,0:T(8,128)(2,1)S(1)} collective-permute-done((bf16[512,512]{1,0:T(8,128)(2,1)S(1)}, bf16[512,512]{1,0:T(8,128)(2,1)S(1)}, u32[]{:S(2)}, u32[]{:S(2)}) %collective-permute-start.28) | collective-permute-done | bytes 524320 | tf_op jit(solution)/shard_map/ppermute | solution.py:28
  177.7 11.9 %collective-permute-start.29 = (bf16[512,512]{1,0:T(8,128)(2,1)S(1)}, bf16[512,512]{1,0:T(8,128)(2,1)S(1)}, u32[]{:S(2)}, u32[]{:S(2)}) collective-permute-start(bf16[512,512]{1,0:T(8,128)(2,1)S(1)} %collective-permute-done.28), channel_id=1, source_target_pairs={{0,4},{4,0},{8,12},{12,8},{16,20},{20,16},{24,28},{28,24},{32,36},... | collective-permute-start | bytes 1572872 | tf_op jit(solution)/shard_map/ppermute | solution.py:28
  189.6 5.3 %collective-permute-start.31 = (bf16[512,512]{1,0:T(8,128)(2,1)S(1)}, bf16[512,512]{1,0:T(8,128)(2,1)S(1)}, u32[]{:S(2)}, u32[]{:S(2)}) collective-permute-start(bf16[512,512]{1,0:T(8,128)(2,1)S(1)} %collective-permute-done.30), channel_id=1, source_target_pairs={{0,4},{4,0},{8,12},{12,8},{16,20},{20,16},{24,28},{28,24},{32,36},... | collective-permute-start | bytes 1572872 | tf_op jit(solution)/shard_map/ppermute | solution.py:28
  197.1 1.6 collective-permute-done.33
  198.9 2.0 copy-done.6
  (78 shorter events, 20.5 us)
Async XLA Ops:
  0.6 9.7 %collective-permute-start = (bf16[1024,512]{1,0:T(8,128)(2,1)}, bf16[1024,512]{1,0:T(8,128)(2,1)S(1)}, u32[]{:S(2)}, u32[]{:S(2)}) collective-permute-start(bf16[1024,512]{1,0:T(8,128)(2,1)} %f_ref.1), channel_id=1, source_target_pairs={{0,4},{4,0},{8,12},{12,8},{16,20},{20,16},{24,28},{28,24},{32,36},... | collective-permute-start | bytes 3145736 | tf_op jit(solution)/shard_map/ppermute | solution.py:28
  1.4 2.2 %copy-start = (bf16[4096,512]{1,0:T(8,128)(2,1)S(1)}, bf16[4096,512]{1,0:T(8,128)(2,1)}, u32[]{:S(2)}) copy-start(bf16[4096,512]{1,0:T(8,128)(2,1)} %c_ref.5) | copy-start | bytes 12582916
  3.6 1.2 copy-start.3
  4.8 5.6 %copy-start.1 = (bf16[4096,512]{1,0:T(8,128)(2,1)S(1)}, bf16[4096,512]{1,0:T(8,128)(2,1)}, u32[]{:S(2)}) copy-start(bf16[4096,512]{1,0:T(8,128)(2,1)} %c_ref.5) | copy-start | bytes 12582916
  4.8 21.7 %copy-start.4 = (bf16[1024,512]{1,0:T(8,128)(2,1)S(1)}, bf16[1024,512]{1,0:T(8,128)(2,1)}, u32[]{:S(2)}) copy-start(bf16[1024,512]{1,0:T(8,128)(2,1)} %f_ref.1) | copy-start | bytes 3145732
  10.4 16.1 %copy-start.5 = (bf16[1024,512]{1,0:T(8,128)(2,1)}, bf16[1024,512]{1,0:T(8,128)(2,1)S(1)}, u32[]{:S(2)}) copy-start(bf16[1024,512]{1,0:T(8,128)(2,1)S(1)} %collective-permute-done.f_ref) | copy-start | bytes 3145732
  16.0 4.0 %collective-permute-start.1 = (f32[1,2048]{1,0:T(1,128)S(1)}, f32[1,2048]{1,0:T(1,128)S(1)}, u32[]{:S(2)}, u32[]{:S(2)}) collective-permute-start(f32[1,2048]{1,0:T(1,128)S(1)} %log_add_fusion.1), channel_id=1, source_target_pairs={{0,32},{4,36},{8,40},{12,44},{16,48},{20,52},{24,56},{28,60},{32,6... | collective-permute-start | bytes 24584 | tf_op jit(solution)/shard_map/ppermute | solution.py:28
  17.3 4.0 %collective-permute-start.2 = (f32[1,2048]{1,0:T(1,128)S(1)}, f32[1,2048]{1,0:T(1,128)S(1)}, u32[]{:S(2)}, u32[]{:S(2)}) collective-permute-start(f32[1,2048]{1,0:T(1,128)S(1)} %log_add_fusion.1), channel_id=1, source_target_pairs={{0,64},{4,68},{8,72},{12,76},{16,80},{20,84},{24,88},{28,92},{32,9... | collective-permute-start | bytes 24584 | tf_op jit(solution)/shard_map/ppermute | solution.py:28
  18.1 3.3 %collective-permute-start.3 = (f32[1,2048]{1,0:T(1,128)S(1)}, f32[1,2048]{1,0:T(1,128)S(1)}, u32[]{:S(2)}, u32[]{:S(2)}) collective-permute-start(f32[1,2048]{1,0:T(1,128)S(1)} %log_add_fusion.1), channel_id=1, source_target_pairs={{0,96},{4,100},{8,104},{12,108},{16,112},{20,116},{24,120},{28,124... | collective-permute-start | bytes 24584 | tf_op jit(solution)/shard_map/ppermute | solution.py:28
  21.4 7.1 %collective-permute-start.4 = (f32[1,2048]{1,0:T(1,128)S(1)}, f32[1,2048]{1,0:T(1,128)S(1)}, u32[]{:S(2)}, u32[]{:S(2)}) collective-permute-start(f32[1,2048]{1,0:T(1,128)S(1)} %log_add_fusion.p0), channel_id=1, source_target_pairs={{0,8},{4,12},{8,16},{12,20},{16,24},{20,28},{24,0},{28,4},{32,40},... | collective-permute-start | bytes 24584 | tf_op jit(solution)/shard_map/ppermute | solution.py:28
  22.8 5.7 %collective-permute-start.5 = (f32[1,2048]{1,0:T(1,128)S(1)}, f32[1,2048]{1,0:T(1,128)S(1)}, u32[]{:S(2)}, u32[]{:S(2)}) collective-permute-start(f32[1,2048]{1,0:T(1,128)S(1)} %log_add_fusion.p0), channel_id=1, source_target_pairs={{0,16},{4,20},{8,24},{12,28},{16,0},{20,4},{24,8},{28,12},{32,48},... | collective-permute-start | bytes 24584 | tf_op jit(solution)/shard_map/ppermute | solution.py:28
  25.4 3.1 %collective-permute-start.6 = (f32[1,2048]{1,0:T(1,128)S(1)}, f32[1,2048]{1,0:T(1,128)S(1)}, u32[]{:S(2)}, u32[]{:S(2)}) collective-permute-start(f32[1,2048]{1,0:T(1,128)S(1)} %log_add_fusion.p0), channel_id=1, source_target_pairs={{0,24},{4,28},{8,0},{12,4},{16,8},{20,12},{24,16},{28,20},{32,56},... | collective-permute-start | bytes 24584 | tf_op jit(solution)/shard_map/ppermute | solution.py:28
  63.1 5.1 %collective-permute-start.7 = (f32[1,2048]{1,0:T(1,128)S(1)}, f32[1,2048]{1,0:T(1,128)S(1)}, u32[]{:S(2)}, u32[]{:S(2)}) collective-permute-start(f32[1,2048]{1,0:T(1,128)S(1)} %get-tuple-element.23), channel_id=1, source_target_pairs={{0,32},{4,36},{8,40},{12,44},{16,48},{20,52},{24,56},{28,60},{32,6... | collective-permute-start | bytes 24584 | tf_op jit(solution)/shard_map/ppermute | solution.py:28
  64.1 4.1 %collective-permute-start.8 = (f32[1,2048]{1,0:T(1,128)S(1)}, f32[1,2048]{1,0:T(1,128)S(1)}, u32[]{:S(2)}, u32[]{:S(2)}) collective-permute-start(f32[1,2048]{1,0:T(1,128)S(1)} %get-tuple-element.23), channel_id=1, source_target_pairs={{0,64},{4,68},{8,72},{12,76},{16,80},{20,84},{24,88},{28,92},{32,9... | collective-permute-start | bytes 24584 | tf_op jit(solution)/shard_map/ppermute | solution.py:28
  66.5 2.8 %collective-permute-start.9 = (f32[1,2048]{1,0:T(1,128)S(1)}, f32[1,2048]{1,0:T(1,128)S(1)}, u32[]{:S(2)}, u32[]{:S(2)}) collective-permute-start(f32[1,2048]{1,0:T(1,128)S(1)} %get-tuple-element.23), channel_id=1, source_target_pairs={{0,96},{4,100},{8,104},{12,108},{16,112},{20,116},{24,120},{28,124... | collective-permute-start | bytes 24584 | tf_op jit(solution)/shard_map/ppermute | solution.py:28
  69.3 3.8 %collective-permute-start.10 = (f32[1,2048]{1,0:T(1,128)S(1)}, f32[1,2048]{1,0:T(1,128)S(1)}, u32[]{:S(2)}, u32[]{:S(2)}) collective-permute-start(f32[1,2048]{1,0:T(1,128)S(1)} %add_add_fusion.1.p0), channel_id=1, source_target_pairs={{0,8},{4,12},{8,16},{12,20},{16,24},{20,28},{24,0},{28,4},{32,40},... | collective-permute-start | bytes 24584 | tf_op jit(solution)/shard_map/ppermute | solution.py:28
  69.5 4.4 %collective-permute-start.11 = (f32[1,2048]{1,0:T(1,128)S(1)}, f32[1,2048]{1,0:T(1,128)S(1)}, u32[]{:S(2)}, u32[]{:S(2)}) collective-permute-start(f32[1,2048]{1,0:T(1,128)S(1)} %add_add_fusion.1.p0), channel_id=1, source_target_pairs={{0,16},{4,20},{8,24},{12,28},{16,0},{20,4},{24,8},{28,12},{32,48},... | collective-permute-start | bytes 24584 | tf_op jit(solution)/shard_map/ppermute | solution.py:28
  72.8 2.8 %collective-permute-start.12 = (f32[1,2048]{1,0:T(1,128)S(1)}, f32[1,2048]{1,0:T(1,128)S(1)}, u32[]{:S(2)}, u32[]{:S(2)}) collective-permute-start(f32[1,2048]{1,0:T(1,128)S(1)} %add_add_fusion.1.p0), channel_id=1, source_target_pairs={{0,24},{4,28},{8,0},{12,4},{16,8},{20,12},{24,16},{28,20},{32,56},... | collective-permute-start | bytes 24584 | tf_op jit(solution)/shard_map/ppermute | solution.py:28
  97.2 4.0 %collective-permute-start.13 = (f32[1,2048]{1,0:T(1,128)S(1)}, f32[1,2048]{1,0:T(1,128)S(1)}, u32[]{:S(2)}, u32[]{:S(2)}) collective-permute-start(f32[1,2048]{1,0:T(1,128)S(1)} %col_sums.1), channel_id=1, source_target_pairs={{0,32},{4,36},{8,40},{12,44},{16,48},{20,52},{24,56},{28,60},{32,6... | collective-permute-start | bytes 24584 | tf_op jit(solution)/shard_map/ppermute | solution.py:28
  98.4 4.0 %collective-permute-start.14 = (f32[1,2048]{1,0:T(1,128)S(1)}, f32[1,2048]{1,0:T(1,128)S(1)}, u32[]{:S(2)}, u32[]{:S(2)}) collective-permute-start(f32[1,2048]{1,0:T(1,128)S(1)} %col_sums.1), channel_id=1, source_target_pairs={{0,64},{4,68},{8,72},{12,76},{16,80},{20,84},{24,88},{28,92},{32,9... | collective-permute-start | bytes 24584 | tf_op jit(solution)/shard_map/ppermute | solution.py:28
  100.8 2.8 %collective-permute-start.15 = (f32[1,2048]{1,0:T(1,128)S(1)}, f32[1,2048]{1,0:T(1,128)S(1)}, u32[]{:S(2)}, u32[]{:S(2)}) collective-permute-start(f32[1,2048]{1,0:T(1,128)S(1)} %col_sums.1), channel_id=1, source_target_pairs={{0,96},{4,100},{8,104},{12,108},{16,112},{20,116},{24,120},{28,124... | collective-permute-start | bytes 24584 | tf_op jit(solution)/shard_map/ppermute | solution.py:28
  103.6 3.8 %collective-permute-start.16 = (f32[1,2048]{1,0:T(1,128)S(1)}, f32[1,2048]{1,0:T(1,128)S(1)}, u32[]{:S(2)}, u32[]{:S(2)}) collective-permute-start(f32[1,2048]{1,0:T(1,128)S(1)} %add_add_fusion.p0), channel_id=1, source_target_pairs={{0,8},{4,12},{8,16},{12,20},{16,24},{20,28},{24,0},{28,4},{32,40},... | collective-permute-start | bytes 24584 | tf_op jit(solution)/shard_map/ppermute | solution.py:28
  103.7 4.1 %collective-permute-start.17 = (f32[1,2048]{1,0:T(1,128)S(1)}, f32[1,2048]{1,0:T(1,128)S(1)}, u32[]{:S(2)}, u32[]{:S(2)}) collective-permute-start(f32[1,2048]{1,0:T(1,128)S(1)} %add_add_fusion.p0), channel_id=1, source_target_pairs={{0,16},{4,20},{8,24},{12,28},{16,0},{20,4},{24,8},{28,12},{32,48},... | collective-permute-start | bytes 24584 | tf_op jit(solution)/shard_map/ppermute | solution.py:28
  105.9 2.5 %collective-permute-start.18 = (f32[1,2048]{1,0:T(1,128)S(1)}, f32[1,2048]{1,0:T(1,128)S(1)}, u32[]{:S(2)}, u32[]{:S(2)}) collective-permute-start(f32[1,2048]{1,0:T(1,128)S(1)} %add_add_fusion.p0), channel_id=1, source_target_pairs={{0,24},{4,28},{8,0},{12,4},{16,8},{20,12},{24,16},{28,20},{32,56},... | collective-permute-start | bytes 24584 | tf_op jit(solution)/shard_map/ppermute | solution.py:28
  114.5 11.7 %all-to-all-start.2 = ((f32[8,1,2048]{2,1,0:T(1,128)}), f32[8,1,2048]{2,1,0:T(1,128)S(1)}, u32[]{:S(2)}, u32[]{:S(2)}) async-start(f32[8,1,2048]{2,1,0:T(1,128)} %get-tuple-element.26), calls=%async_computation.2 | async-start | bytes 131072 | tf_op jit(solution)/shard_map/all_to_all | solution.py:385
  126.2 1.6 copy-start.2
  131.4 13.6 %collective-permute-start.21 = (bf16[528,512]{1,0:T(8,128)(2,1)S(1)}, bf16[528,512]{1,0:T(8,128)(2,1)}, u32[]{:S(2)}, u32[]{:S(2)}) collective-permute-start(bf16[528,512]{1,0:T(8,128)(2,1)S(1)} %numerators.7), channel_id=1, source_target_pairs={{0,24},{4,100},{8,0},{12,108},{16,8},{20,116},{24,16},{28,124},{32... | collective-permute-start | bytes 1622024 | tf_op jit(solution)/shard_map/ppermute | solution.py:28
  134.6 10.5 %collective-permute-start.20 = (bf16[528,512]{1,0:T(8,128)(2,1)S(1)}, bf16[528,512]{1,0:T(8,128)(2,1)}, u32[]{:S(2)}, u32[]{:S(2)}) collective-permute-start(bf16[528,512]{1,0:T(8,128)(2,1)S(1)} %numerators.6), channel_id=1, source_target_pairs={{0,8},{4,36},{8,16},{12,44},{16,24},{20,52},{24,0},{28,60},{32,40}... | collective-permute-start | bytes 1622024 | tf_op jit(solution)/shard_map/ppermute | solution.py:28
  139.2 10.4 %collective-permute-start.19 = (bf16[528,512]{1,0:T(8,128)(2,1)}, bf16[528,512]{1,0:T(8,128)(2,1)}, u32[]{:S(2)}, u32[]{:S(2)}) collective-permute-start(bf16[528,512]{1,0:T(8,128)(2,1)} %numerators.5), channel_id=1, source_target_pairs={{0,16},{4,68},{8,24},{12,76},{16,0},{20,84},{24,8},{28,92},{32,48}... | collective-permute-start | bytes 1622024 | tf_op jit(solution)/shard_map/ppermute | solution.py:28
  151.3 5.5 %collective-permute-start.22 = (bf16[528,128]{1,0:T(8,128)(2,1)S(1)}, bf16[528,128]{1,0:T(8,128)(2,1)S(1)}, u32[]{:S(2)}, u32[]{:S(2)}) collective-permute-start(bf16[528,128]{1,0:T(8,128)(2,1)S(1)} %get-tuple-element.30), channel_id=1, source_target_pairs={{0,64},{4,20},{8,72},{12,28},{16,80},{20,4},{24,88},{28,12},{32,96... | collective-permute-start | bytes 405512 | tf_op jit(solution)/shard_map/ppermute | solution.py:28
  152.6 5.6 %collective-permute-start.23 = (bf16[528,128]{1,0:T(8,128)(2,1)S(1)}, bf16[528,128]{1,0:T(8,128)(2,1)S(1)}, u32[]{:S(2)}, u32[]{:S(2)}) collective-permute-start(bf16[528,128]{1,0:T(8,128)(2,1)S(1)} %get-tuple-element.31), channel_id=1, source_target_pairs={{0,32},{4,12},{8,40},{12,20},{16,48},{20,28},{24,56},{28,4},{32,64... | collective-permute-start | bytes 405512 | tf_op jit(solution)/shard_map/ppermute | solution.py:28
  154.2 4.0 %collective-permute-start.24 = (bf16[528,128]{1,0:T(8,128)(2,1)S(1)}, bf16[528,128]{1,0:T(8,128)(2,1)S(1)}, u32[]{:S(2)}, u32[]{:S(2)}) collective-permute-start(bf16[528,128]{1,0:T(8,128)(2,1)S(1)} %get-tuple-element.32), channel_id=1, source_target_pairs={{0,96},{4,28},{8,104},{12,4},{16,112},{20,12},{24,120},{28,20},{32... | collective-permute-start | bytes 405512 | tf_op jit(solution)/shard_map/ppermute | solution.py:28
  158.4 5.1 %collective-permute-start.25 = (bf16[128,512]{1,0:T(8,128)(2,1)S(1)}, bf16[128,512]{1,0:T(8,128)(2,1)S(1)}, u32[]{:S(2)}, u32[]{:S(2)}) collective-permute-start(bf16[128,512]{1,0:T(8,128)(2,1)S(1)} %add_second.1), channel_id=1, source_target_pairs={{0,32},{4,12},{8,40},{12,20},{16,48},{20,28},{24,56},{28,4},{32,64... | collective-permute-start | bytes 393224 | tf_op jit(solution)/shard_map/ppermute | solution.py:28
  159.7 5.9 %collective-permute-start.26 = (bf16[128,512]{1,0:T(8,128)(2,1)S(1)}, bf16[128,512]{1,0:T(8,128)(2,1)S(1)}, u32[]{:S(2)}, u32[]{:S(2)}) collective-permute-start(bf16[128,512]{1,0:T(8,128)(2,1)S(1)} %add_second.1), channel_id=1, source_target_pairs={{0,64},{4,20},{8,72},{12,28},{16,80},{20,4},{24,88},{28,12},{32,96... | collective-permute-start | bytes 393224 | tf_op jit(solution)/shard_map/ppermute | solution.py:28
  161.9 3.8 %collective-permute-start.27 = (bf16[128,512]{1,0:T(8,128)(2,1)S(1)}, bf16[128,512]{1,0:T(8,128)(2,1)S(1)}, u32[]{:S(2)}, u32[]{:S(2)}) collective-permute-start(bf16[128,512]{1,0:T(8,128)(2,1)S(1)} %add_second.1), channel_id=1, source_target_pairs={{0,96},{4,28},{8,104},{12,4},{16,112},{20,12},{24,120},{28,20},{32... | collective-permute-start | bytes 393224 | tf_op jit(solution)/shard_map/ppermute | solution.py:28
  165.7 12.0 %collective-permute-start.28 = (bf16[512,512]{1,0:T(8,128)(2,1)S(1)}, bf16[512,512]{1,0:T(8,128)(2,1)S(1)}, u32[]{:S(2)}, u32[]{:S(2)}) collective-permute-start(bf16[512,512]{1,0:T(8,128)(2,1)S(1)} %constant_dynamic-update-slice_fusion.8), channel_id=1, source_target_pairs={{0,16},{4,68},{8,24},{12,76},{16,0},{20,84},{24,8},{28,92},{32,48}... | collective-permute-start | bytes 1572872 | tf_op jit(solution)/shard_map/ppermute | solution.py:28
  169.3 20.2 %collective-permute-start.30 = (bf16[512,512]{1,0:T(8,128)(2,1)S(1)}, bf16[512,512]{1,0:T(8,128)(2,1)S(1)}, u32[]{:S(2)}, u32[]{:S(2)}) collective-permute-start(bf16[512,512]{1,0:T(8,128)(2,1)S(1)} %constant_dynamic-update-slice_fusion.8), channel_id=1, source_target_pairs={{0,8},{4,36},{8,16},{12,44},{16,24},{20,52},{24,0},{28,60},{32,40}... | collective-permute-start | bytes 1572872 | tf_op jit(solution)/shard_map/ppermute | solution.py:28
  170.5 25.6 %collective-permute-start.32 = (bf16[512,512]{1,0:T(8,128)(2,1)S(1)}, bf16[512,512]{1,0:T(8,128)(2,1)S(1)}, u32[]{:S(2)}, u32[]{:S(2)}) collective-permute-start(bf16[512,512]{1,0:T(8,128)(2,1)S(1)} %constant_dynamic-update-slice_fusion.8), channel_id=1, source_target_pairs={{0,24},{4,100},{8,0},{12,108},{16,8},{20,116},{24,16},{28,124},{32... | collective-permute-start | bytes 1572872 | tf_op jit(solution)/shard_map/ppermute | solution.py:28
  177.7 19.2 %collective-permute-start.29 = (bf16[512,512]{1,0:T(8,128)(2,1)S(1)}, bf16[512,512]{1,0:T(8,128)(2,1)S(1)}, u32[]{:S(2)}, u32[]{:S(2)}) collective-permute-start(bf16[512,512]{1,0:T(8,128)(2,1)S(1)} %collective-permute-done.28), channel_id=1, source_target_pairs={{0,4},{4,0},{8,12},{12,8},{16,20},{20,16},{24,28},{28,24},{32,36},... | collective-permute-start | bytes 1572872 | tf_op jit(solution)/shard_map/ppermute | solution.py:28
  189.5 5.3 %collective-permute-start.35 = (f32[1,2048]{1,0:T(1,128)S(1)}, f32[1,2048]{1,0:T(1,128)S(1)}, u32[]{:S(2)}, u32[]{:S(2)}) collective-permute-start(f32[1,2048]{1,0:T(1,128)S(1)} %get-tuple-element.34), channel_id=1, source_target_pairs={{0,4},{4,0},{8,12},{12,8},{16,20},{20,16},{24,28},{28,24},{32,36},... | collective-permute-start | bytes 24584 | tf_op jit(solution)/shard_map/ppermute | solution.py:28
  189.6 7.5 %collective-permute-start.31 = (bf16[512,512]{1,0:T(8,128)(2,1)S(1)}, bf16[512,512]{1,0:T(8,128)(2,1)S(1)}, u32[]{:S(2)}, u32[]{:S(2)}) collective-permute-start(bf16[512,512]{1,0:T(8,128)(2,1)S(1)} %collective-permute-done.30), channel_id=1, source_target_pairs={{0,4},{4,0},{8,12},{12,8},{16,20},{20,16},{24,28},{28,24},{32,36},... | collective-permute-start | bytes 1572872 | tf_op jit(solution)/shard_map/ppermute | solution.py:28
  196.1 2.8 %collective-permute-start.34 = (bf16[512,512]{1,0:T(8,128)(2,1)S(1)}, bf16[512,512]{1,0:T(8,128)(2,1)S(1)}, u32[]{:S(2)}, u32[]{:S(2)}) collective-permute-start(bf16[512,512]{1,0:T(8,128)(2,1)S(1)} %constant_dynamic-update-slice_fusion.8), channel_id=1, source_target_pairs={{0,4},{4,0},{8,12},{12,8},{16,20},{20,16},{24,28},{28,24},{32,36},... | collective-permute-start | bytes 1572872 | tf_op jit(solution)/shard_map/ppermute | solution.py:28
  196.1 2.7 %collective-permute-start.33 = (bf16[512,512]{1,0:T(8,128)(2,1)S(1)}, bf16[512,512]{1,0:T(8,128)(2,1)S(1)}, u32[]{:S(2)}, u32[]{:S(2)}) collective-permute-start(bf16[512,512]{1,0:T(8,128)(2,1)S(1)} %collective-permute-done.32), channel_id=1, source_target_pairs={{0,4},{4,0},{8,12},{12,8},{16,20},{20,16},{24,28},{28,24},{32,36},... | collective-permute-start | bytes 1572872 | tf_op jit(solution)/shard_map/ppermute | solution.py:28
  198.9 2.0 %copy-start.6 = (bf16[4096,512]{1,0:T(8,128)(2,1)}, bf16[4096,512]{1,0:T(8,128)(2,1)S(1)}, u32[]{:S(2)}) copy-start(bf16[4096,512]{1,0:T(8,128)(2,1)S(1)} %constant_dynamic-update-slice_fusion) | copy-start | bytes 12582916
